TPU v7x, 128 devices: a whole 4x4x4 slice. The times are simulated.
128 devices in a mesh: gx: 16 (over x, z), gy: 4 (over y_lo, core), gz: 2 (over y_hi).
Axes of the slice: x: 4, y: 4 (y_hi: 2, y_lo: 2; y = y_hi * 2 + y_lo), z: 4, core: 2. Of those that a mesh axis runs over, the one named last changes fastest.
Arguments:
- courant: float32 [512, 256, 512], P('gx', 'gy', 'gz'), may hold values from 0.06 to 0.19
- current: float32 [512, 256, 512], P('gx', 'gy', 'gz'), may hold values from -3 to 9
- previous: float32 [512, 256, 512], P('gx', 'gy', 'gz'), may hold values from -3 to 9
- image_in: float32 [512, 256, 512], P('gx', 'gy', 'gz'), may hold values from -6 to 6
- forward_tt: float32 [4, 512, 256, 512], P(None, 'gx', 'gy', 'gz'), may hold values from -4 to 4
- traces: float32 [32768, 4], P(('gx', 'gy', 'gz')), may hold values from -8 to 8
- trace_owner: int32 [32768, 1], P(('gx', 'gy', 'gz')), may hold values from 0 to 127; in each aligned block of 256 rows (0 to 255, 256 to 511, ...) at most 8 rows name the same one
- receiver_cell: int32 [32768], P(('gx', 'gy', 'gz')), may hold values from 0 to 524287
Outputs:
- image: float32 [512, 256, 512], P('gx', 'gy', 'gz')
- final_now: float32 [512, 256, 512], P('gx', 'gy', 'gz')
- final_before: float32 [512, 256, 512], P('gx', 'gy', 'gz')
Inputs may be any that keep to these rules, and one draw needn't show every extreme that they name: `trace_owner`: tiles are numbered in gx, gy, gz order. Among the 256 rows of one device (aligned blocks), no tile is named by more than 8 rows, a bound that some block reaches. `receiver_cell`: cell x * 64 * 256 + y * 256 + z of the owner's tile.
All inputs are finite; a program needn't handle non-finite values.
Results may differ from a plain program's by a relative error of at most 0.00002.
Values sent between devices are 32-bit elements; how exact they have to be, the bound alone decides.
A program may use at most 384 MiB of HBM per device.

v0:
```python
from types import SimpleNamespace

import jax
import jax.numpy as jnp
from jax import lax
from jax.experimental import pallas as pl
from jax.experimental.pallas import tpu as pltpu
from jax.sharding import PartitionSpec as P

STEPS = 4
CAP = 8
CX, CY, CZ = 32, 64, 256
N_GX, N_GY, N_GZ = 16, 4, 2
RECS = 256
ROWS = 16
CHUNKS = (1, 2, 0, 3)
SCALE = 5040.0
TAPS = (0.0, 8064.0, -1008.0, 128.0, -9.0)
CENTRE = -43050.0
F32, BF16, I32 = jnp.float32, jnp.bfloat16, jnp.int32
MESH = pl.DeviceIdType.MESH


def split(v):
    hi = v.astype(BF16)
    return hi, (v - hi.astype(F32)).astype(BF16)


def tap_of(distance):
    out = jnp.zeros(distance.shape, F32)
    for offset in range(1, 5):
        out = jnp.where(distance == offset, TAPS[offset], out)
    return out


def dot(a, b):
    return lax.dot_general(a, b, (((1,), (0,)), ((), ())), preferred_element_type=F32)


def iota(shape, dim):
    return lax.broadcasted_iota(I32, shape, dim)


PARTS = ((0, 7), (1, 2, 3, 4, 5, 6))
PAIRS = ((0, 1, 14, 15), tuple(range(2, 14)))
Y_ROWS = ((0, 32), (32, 96))
TILE = (CX, CY, CZ)
MIB = 1024 * 1024


def pick_from(values, i):
    out = i + values[0]
    for n in range(1, len(values)):
        if values[n] != values[n - 1] + 1:
            out = jnp.where(i >= n, i - n + values[n], out)
    return out


def edges(n, shift, downward):
    r_, c_ = iota((n, n), 0), iota((n, n), 1)
    same = (c_ // 4) == lax.rem(r_ // 4 + shift, n // 4)
    gap = lax.rem(r_, 4) - lax.rem(c_, 4)
    gap = jnp.where(downward, gap, -gap)
    return jnp.where(same & (gap >= 0), tap_of(4 - gap), 0.0)


def place():
    at = SimpleNamespace(gx=lax.axis_index("gx"), gy=lax.axis_index("gy"), gz=lax.axis_index("gz"))
    at.right, at.left = at.gx < N_GX - 1, at.gx > 0
    at.up, at.down = at.gy < N_GY - 1, at.gy > 0
    return at


def faces(at, ys, yr, zs, zr, ys_sem, yr_sem, zs_sem, zr_sem, weights):
    band_z, band_y, edge_y, edge_y_few, edge_z = weights
    block_of_lane = iota((CY, 128), 1) // 4
    own_block = lax.rem(block_of_lane + 32 - at.gz, 32)
    inside = block_of_lane == 31 * (1 - at.gz)
    row8 = iota((8, CZ), 0)
    half = pl.ds(pl.multiple_of((1 - at.gz) * 128, 128), 128)

    def y_copy(n, part, side):
        rows = pl.ds(*Y_ROWS[part])
        return pltpu.make_async_remote_copy(
            src_ref=ys.at[n, side, rows], dst_ref=yr.at[n, side, rows],
            send_sem=ys_sem.at[n, part, side], recv_sem=yr_sem.at[n, part, side],
            device_id=(at.gx, at.gy + 1 if side == 0 else at.gy - 1, at.gz), device_id_type=MESH)

    def z_copy(n, part):
        return pltpu.make_async_remote_copy(
            src_ref=zs.at[n, part], dst_ref=zr.at[n, part],
            send_sem=zs_sem.at[n, part], recv_sem=zr_sem.at[n, part],
            device_id=(at.gx, at.gy, 1 - at.gz), device_id_type=MESH)

    def clear(slots):
        @pl.when(at.gy == 0)
        def _():
            for n in range(slots):
                yr[n, 0] = jnp.zeros(yr.shape[2:], F32)

        @pl.when(at.gy == N_GY - 1)
        def _():
            for n in range(slots):
                yr[n, 1] = jnp.zeros(yr.shape[2:], F32)

    def send(n, part, v):
        first, count = Y_ROWS[part]
        packed_rows = []
        for p in PAIRS[part]:
            a, b = v[2 * p, CY - 8:CY, :], v[2 * p + 1, CY - 8:CY, :]
            packed_rows.append(jnp.where(row8 < 4, pltpu.roll(a, 4, 0), b))
        for p in PAIRS[part]:
            a, b = v[2 * p, 0:8, :], v[2 * p + 1, 0:8, :]
            packed_rows.append(jnp.where(row8 < 4, a, pltpu.roll(b, 4, 0)))
        hi, lo = split(jnp.concatenate(packed_rows, axis=0))
        matrix = edge_y[...] if part else edge_y_few[...]
        sums = dot(matrix, hi) + dot(matrix, lo)
        for side in range(2):
            ys[n, side, first:first + count, :] = sums[side * count:(side + 1) * count]
        pl.when(at.up)(lambda: y_copy(n, part, 0).start())
        pl.when(at.down)(lambda: y_copy(n, part, 1).start())

        edge = jnp.zeros((CY, 128), F32)
        for g in PARTS[part]:
            for x in range(4 * g, 4 * g + 4):
                moved = pltpu.roll(v[x, :, half], (4 * x + 4) % 128, 1)
                edge = jnp.where(own_block == x, moved, edge)
        hi, lo = split(edge)
        zs[n, part] = dot(hi, edge_z[...]) + dot(lo, edge_z[...])
        z_copy(n, part).start()

    def add(n, part, total):
        pl.when(at.down)(lambda: y_copy(n, part, 0).wait_recv())
        pl.when(at.up)(lambda: y_copy(n, part, 1).wait_recv())
        first, count = Y_ROWS[part]
        for i, p in enumerate(PAIRS[part]):
            top = yr[n, 0, first + i * 8:first + i * 8 + 8, :]
            end = yr[n, 1, first + i * 8:first + i * 8 + 8, :]
            total[2 * p, 0:8, :] += jnp.where(row8 < 4, top, 0.0)
            total[2 * p + 1, 0:8, :] += jnp.where(row8 < 4, pltpu.roll(top, 4, 0), 0.0)
            total[2 * p, CY - 8:CY, :] += jnp.where(row8 < 4, 0.0, pltpu.roll(end, 4, 0))
            total[2 * p + 1, CY - 8:CY, :] += jnp.where(row8 < 4, 0.0, end)
        z_copy(n, part).wait_recv()
        got = zr[n, part]
        for g in PARTS[part]:
            for x in range(4 * g, 4 * g + 4):
                moved = pltpu.roll(got, (128 - 4 * x) % 128, 1)
                total[x, :, half] += jnp.where(inside, moved, 0.0)

    def wait_sent(slots):
        for n in range(slots):
            for part in range(2):
                pl.when(at.up)(lambda: y_copy(n, part, 0).wait_send())
                pl.when(at.down)(lambda: y_copy(n, part, 1).wait_send())
                z_copy(n, part).wait_send()

    def bands(part, v_at, total):
        def body(i, carry):
            g = pick_from(PARTS[part], i)
            v = v_at[pl.ds(4 * g, 4)].reshape(4 * CY, CZ)
            hi, lo = split(v)
            here = dot(hi, band_z[...]) + dot(lo, band_z[...]) + CENTRE * v
            for p in range(4):
                rows = slice(p * CY, (p + 1) * CY)
                both = jnp.concatenate([hi[rows], lo[rows]], axis=0)
                total[4 * g + p] = here[rows] + dot(band_y[...], both)
            return carry
        lax.fori_loop(0, len(PARTS[part]), body, 0)

    return SimpleNamespace(clear=clear, send=send, add=add, wait_sent=wait_sent, bands=bands)


def x_copy(at, src, dst, sems, k, c, side):
    rows = pl.ds(c * ROWS, ROWS)
    planes = pl.ds(CX - 4, 4) if side == 0 else pl.ds(0, 4)
    return pltpu.make_async_remote_copy(
        src_ref=src.at[planes, rows], dst_ref=dst.at[side, :, rows],
        send_sem=sems[0].at[k, c, side], recv_sem=sems[1].at[k, c, side],
        device_id=(at.gx + 1 if side == 0 else at.gx - 1, at.gy, at.gz), device_id_type=MESH)


def first_kernel(current, previous, courant, image_in, traces, owners, cells,
                 cur, prev, cou, img, total, halo, values, targets,
                 band_z, band_y, edge_y, edge_y_few, edge_z,
                 tr, ow, ce, packed, r1, t1, r2, ys, yr, zs, zr,
                 in_sem, xs_sem, xr_sem, ys_sem, yr_sem, zs_sem, zr_sem, route_sem):
    at = place()
    group = at.gy * N_GZ + at.gz
    loads = [
        pltpu.make_async_copy(traces, tr, in_sem.at[0]),
        pltpu.make_async_copy(owners, ow, in_sem.at[1]),
        pltpu.make_async_copy(cells, ce, in_sem.at[2]),
        pltpu.make_async_copy(current, cur, in_sem.at[3]),
        pltpu.make_async_copy(courant, cou, in_sem.at[4]),
        pltpu.make_async_copy(previous, prev, in_sem.at[5]),
        pltpu.make_async_copy(image_in, img, in_sem.at[6]),
    ]
    for load in loads:
        load.start()

    barrier = pltpu.get_barrier_semaphore()

    def in_group(offset):
        other = lax.rem(group + offset, N_GY * N_GZ)
        return other, (at.gx, other // N_GZ, lax.rem(other, N_GZ))

    def in_line(offset):
        other = lax.rem(at.gx + offset, N_GX)
        return other, (other, at.gy, at.gz)

    def greet_group(o, carry):
        pl.semaphore_signal(barrier, inc=1, device_id=in_group(o)[1], device_id_type=MESH)
        return carry

    def greet_line(o, carry):
        pl.semaphore_signal(barrier, inc=1, device_id=in_line(o)[1], device_id_type=MESH)
        return carry

    lax.fori_loop(1, 16, greet_line, 0)
    lax.fori_loop(1, 8, greet_group, 0)

    for load in loads[:3]:
        load.wait()
    owner = ow[...]
    cell = ce[...]
    row = cell // CZ
    field = [None] * 16
    for k in range(STEPS):
        hi, lo = split(tr[k:k + 1, :] * SCALE)
        field[k], field[4 + k] = hi.astype(F32), lo.astype(F32)
    field[8] = (row // 256).astype(F32)
    field[9] = (row % 256).astype(F32)
    field[10] = (cell % CZ).astype(F32)
    field[11] = jnp.ones((1, RECS), F32)
    zero = jnp.zeros((1, RECS), F32)
    field = jnp.concatenate([zero if f is None else f for f in field], axis=0)
    fields = jnp.concatenate([field] * 8, axis=0)
    owner_f = owner.astype(F32)
    owner_col = jnp.transpose(jnp.broadcast_to(owner_f, (128, RECS)))[:, :1]
    earlier = (owner_col == owner_f) & (iota((RECS, RECS), 0) < iota((RECS, RECS), 1))
    rank = jnp.sum(jnp.where(earlier, 1.0, 0.0), axis=0, keepdims=True)
    mine = iota((128, RECS), 0) == owner
    lane_block = iota((128, RECS), 0) // 16
    sums = jnp.zeros((128, 128), F32)
    for j in range(CAP):
        pick = jnp.where(mine & (rank == float(j)), 1.0, 0.0).astype(BF16)
        part = jnp.where(lane_block == j, fields, 0.0).astype(BF16)
        sums = sums + lax.dot_general(pick, part, (((1,), (1,)), ((), ())), preferred_element_type=F32)
    packed[...] = sums.reshape(16, 8, 128)

    pl.semaphore_wait(barrier, 22)

    def send_line(o, carry):
        other, device = in_line(o)
        pltpu.make_async_remote_copy(
            src_ref=packed.at[other], dst_ref=r1.at[o], send_sem=route_sem.at[0], recv_sem=route_sem.at[1],
            device_id=device, device_id_type=MESH).start()
        return carry

    lax.fori_loop(1, 16, send_line, 0)

    def x_face(c, side):
        return x_copy(at, current, halo, (xs_sem, xr_sem), 0, c, side)

    for c in CHUNKS:
        pl.when(at.right)(lambda: x_face(c, 0).start())
        pl.when(at.left)(lambda: x_face(c, 1).start())
    r1[0] = packed[at.gx]

    r_, c_ = iota((CZ, CZ), 0), iota((CZ, CZ), 1)
    band_z[...] = tap_of(jnp.abs(r_ - c_)).astype(BF16)
    r_, c_ = iota((CY, 2 * CY), 0), iota((CY, 2 * CY), 1)
    band_y[...] = tap_of(jnp.abs(r_ - lax.rem(c_, CY))).astype(BF16)
    edge_z[...] = edges(128, 30 * at.gz, at.gz == 0).astype(BF16)
    for matrix, n in ((edge_y_few, 64), (edge_y, 192)):
        upward = iota((n, n), 0) < n // 2
        matrix[...] = edges(n, 0, ~upward).astype(BF16)

    face = faces(at, ys, yr, zs, zr, ys_sem, yr_sem, zs_sem, zr_sem,
                 (band_z, band_y, edge_y, edge_y_few, edge_z))
    face.clear(1)
    pl.when(~at.left)(lambda: halo.__setitem__(0, jnp.zeros(halo.shape[1:], F32)))
    pl.when(~at.right)(lambda: halo.__setitem__(1, jnp.zeros(halo.shape[1:], F32)))

    loads[3].wait()
    face.send(0, 0, cur)
    face.send(0, 1, cur)

    pltpu.make_async_copy(r1.at[pl.ds(1, 15)], r1.at[pl.ds(1, 15)], route_sem.at[1]).wait()
    for j in range(8):
        t1[j] = r1[:, j, :]

    def send_group(o, carry):
        other, device = in_group(o)
        pltpu.make_async_remote_copy(
            src_ref=t1.at[other], dst_ref=r2.at[o], send_sem=route_sem.at[2], recv_sem=route_sem.at[3],
            device_id=device, device_id_type=MESH).start()
        return carry

    lax.fori_loop(1, 8, send_group, 0)
    r2[0] = t1[group]

    face.bands(0, cur, total)
    face.bands(1, cur, total)
    loads[4].wait()

    def rescale(x, carry):
        cou[x] = cou[x] * (1.0 / SCALE)
        return carry
    lax.fori_loop(0, CX, rescale, 0)
    face.add(0, 0, total)
    face.add(0, 1, total)

    pltpu.make_async_copy(r2.at[pl.ds(1, 7)], r2.at[pl.ds(1, 7)], route_sem.at[3]).wait()
    got = jnp.transpose(r2[...].reshape(128, 128))
    for r in range(CAP):
        values[4 * r:4 * r + 4, :] = got[16 * r:16 * r + 4] + got[16 * r + 4:16 * r + 8]
        cell_row = (got[16 * r + 8:16 * r + 9] * 256.0 + got[16 * r + 9:16 * r + 10]).astype(I32)
        depth = got[16 * r + 10:16 * r + 11].astype(I32)
        targets[r:r + 1, :] = (cell_row // CY) * (2 * CY) + (depth // 128) * CY + cell_row % CY
        targets[CAP + r:CAP + r + 1, :] = depth % 128
    held = got[11:12]
    for r in range(1, CAP):
        held = held + got[16 * r + 11:16 * r + 12]
    targets[2 * CAP:2 * CAP + 1, :] = held.astype(I32)
    targets[2 * CAP + 1:, :] = jnp.zeros((7, 128), I32)

    for load in loads[5:]:
        load.wait()
    for c in CHUNKS:
        pl.when(at.left)(lambda: x_face(c, 0).wait_recv())
        pl.when(at.right)(lambda: x_face(c, 1).wait_recv())
        pl.when(at.right)(lambda: x_face(c, 0).wait_send())
        pl.when(at.left)(lambda: x_face(c, 1).wait_send())
    pltpu.make_async_copy(r1.at[pl.ds(1, 15)], r1.at[pl.ds(1, 15)], route_sem.at[0]).wait()
    pltpu.make_async_copy(r2.at[pl.ds(1, 7)], r2.at[pl.ds(1, 7)], route_sem.at[2]).wait()
    face.wait_sent(1)


def source_kernel(values, targets, source, field, spread, where, sem):
    fetch = pltpu.make_async_copy(targets, where, sem)
    fetch.start()
    rows = field.reshape(CX * 2 * CY * STEPS, 128)

    def blank(i, carry):
        rows[pl.ds(pl.multiple_of(i * 512, 512), 512), :] = jnp.zeros((512, 128), F32)
        return carry
    lax.fori_loop(0, CX * 2 * CY * STEPS // 512, blank, 0)
    for p in range(128):
        spread[p] = jnp.broadcast_to(values[:, p:p + 1], (CAP * STEPS, 128))
    fetch.wait()
    lanes = iota((STEPS, 128), 1)

    def put(entries):
        row = [where[r, p] for p, r in entries]
        part = [jnp.where(lanes == where[CAP + r, p], spread[p, STEPS * r:STEPS * (r + 1), :], 0.0) for p, r in entries]
        old = [field[i] for i in row]
        for i in range(len(entries)):
            total = old[i] + part[i]
            for j in range(len(entries)):
                if j != i:
                    total = total + jnp.where(row[i] == row[j], part[j], 0.0)
            old[i] = total
        for i in range(len(entries)):
            field[row[i]] = old[i]

    def two(i, carry):
        a, b = 2 * i, 2 * i + 1
        put(((a, 0), (a, 1), (b, 0), (b, 1)))

        @pl.when((where[2 * CAP, a] > 2) | (where[2 * CAP, b] > 2))
        def _():
            put(((a, 2), (a, 3), (b, 2), (b, 3)))

            @pl.when((where[2 * CAP, a] > 4) | (where[2 * CAP, b] > 4))
            def _():
                put(((a, 4), (a, 5), (b, 4), (b, 5)))
                put(((a, 6), (a, 7), (b, 6), (b, 7)))
        return carry
    lax.fori_loop(0, 64, two, 0)

    def arrange(x, carry):
        for k in range(STEPS):
            for h in range(2):
                for t in range(CY // 8):
                    first = ((x * 2 + h) * CY + t * 8) * STEPS + k
                    source[k, x, 8 * t:8 * t + 8, 128 * h:128 * h + 128] = rows[pl.ds(first, 8, stride=STEPS), :]
        return carry
    lax.fori_loop(0, CX, arrange, 0)


def update(planes, rows, window, before, after, cou, fwd, image, image_after, totals):
    for x in planes:
        v = window(x)
        total = totals[0][x, rows, :]
        for more in totals[1:]:
            total = total + more[x, rows, :]
        for o in range(1, 5):
            total = total + TAPS[o] * (window(x - o) + window(x + o))
        new = (v + v) - before[x, rows, :] + cou[x, rows, :] * total
        after[x, rows, :] = new
        image_after[x, rows, :] = image[x, rows, :] + fwd[x, rows, :] * new


def inner(v, *rest):
    def body(t, carry):
        rows = pl.ds(pl.multiple_of(t * 8, 8), 8)
        planes = {x: v[x, rows, :] for x in range(CX)}
        update(range(4, CX - 4), rows, lambda x: planes[x], *rest)
        return carry
    lax.fori_loop(0, CY // 8, body, 0)


def outer(c, halo, v, *rest):
    def body(t, carry):
        rows = pl.ds(pl.multiple_of(t * 8, 8), 8)
        for side in range(2):
            low = 0 if side == 0 else CX - 8
            planes = {x: v[x, rows, :] for x in range(low, low + 8)}
            for i in range(4):
                planes[i - 4 if side == 0 else CX + i] = halo[side, i, rows, :]
            here = range(0, 4) if side == 0 else range(CX - 4, CX)
            update(here, rows, lambda x: planes[x], *rest)
        return carry
    lax.fori_loop(c * ROWS // 8, (c + 1) * ROWS // 8, body, 0)


def step_kernel(cur, prev, cou, img_in, forward, total0, halo0, source, band_z, band_y, edge_y, edge_y_few, edge_z,
                now2, now3, total, img, halo3, fwd3,
                fwd, now1, halos, ys, yr, zs, zr,
                in_sem, xs_sem, xr_sem, ys_sem, yr_sem, zs_sem, zr_sem):
    at = place()
    loads = [pltpu.make_async_copy(forward.at[k], fwd3 if k == STEPS - 1 else fwd.at[k], in_sem.at[k]) for k in range(STEPS)]
    for load in loads:
        load.start()
    barrier = pltpu.get_barrier_semaphore()

    def greet(x, y, z):
        pl.semaphore_signal(barrier, inc=1, device_id=(x, y, z), device_id_type=MESH)

    pl.when(at.right)(lambda: greet(at.gx + 1, at.gy, at.gz))
    pl.when(at.left)(lambda: greet(at.gx - 1, at.gy, at.gz))
    pl.when(at.up)(lambda: greet(at.gx, at.gy + 1, at.gz))
    pl.when(at.down)(lambda: greet(at.gx, at.gy - 1, at.gz))
    greet(at.gx, at.gy, 1 - at.gz)
    one = lambda yes: jnp.where(yes, 1, 0)
    neighbours = 1 + one(at.right) + one(at.left) + one(at.up) + one(at.down)

    v_at = [prev, cur, now1, now2, now3]
    halo = [halo0, halos.at[0], halos.at[1], halo3]
    face = faces(at, ys, yr, zs, zr, ys_sem, yr_sem, zs_sem, zr_sem,
                 (band_z, band_y, edge_y, edge_y_few, edge_z))

    def rest(k):
        totals = (total0, source.at[0]) if k == 0 else (total, source.at[k])
        return (v_at[k], v_at[k + 2], cou, fwd.at[k], img_in if k == 0 else img, img, totals)

    def x_face(k, c, side):
        return x_copy(at, v_at[k + 1], halo[k], (xs_sem, xr_sem), k - 1, c, side)

    def x_start(k, c):
        pl.when(at.right)(lambda: x_face(k, c, 0).start())
        pl.when(at.left)(lambda: x_face(k, c, 1).start())

    def x_wait(k, c):
        pl.when(at.left)(lambda: x_face(k, c, 0).wait_recv())
        pl.when(at.right)(lambda: x_face(k, c, 1).wait_recv())

    face.clear(STEPS - 1)
    for k in range(1, STEPS):
        pl.when(~at.left)(lambda: halo[k].__setitem__(0, jnp.zeros(halo3.shape[1:], F32)))
        pl.when(~at.right)(lambda: halo[k].__setitem__(1, jnp.zeros(halo3.shape[1:], F32)))

    loads[0].wait()
    for c in CHUNKS:
        outer(c, halo0, cur, *rest(0))
    pl.semaphore_wait(barrier, neighbours)
    for c in CHUNKS:
        x_start(1, c)
    face.send(0, 0, now1)
    inner(cur, *rest(0))
    for k in range(1, STEPS - 1):
        v = v_at[k + 1]
        face.send(k - 1, 1, v)
        face.bands(0, v, total)
        face.add(k - 1, 0, total)
        loads[k].wait()
        for c in CHUNKS:
            x_wait(k, c)
            outer(c, halo[k], v, *rest(k))
            x_start(k + 1, c)
        face.send(k, 0, v_at[k + 2])
        face.bands(1, v, total)
        face.add(k - 1, 1, total)
        inner(v, *rest(k))
    last = STEPS - 2
    face.send(last, 1, now3)
    face.bands(0, now3, total)
    face.bands(1, now3, total)
    face.add(last, 0, total)
    face.add(last, 1, total)
    loads[STEPS - 1].wait()
    for c in CHUNKS:
        x_wait(STEPS - 1, c)
    for k in range(1, STEPS):
        for c in CHUNKS:
            pl.when(at.right)(lambda: x_face(k, c, 0).wait_send())
            pl.when(at.left)(lambda: x_face(k, c, 1).wait_send())
    face.wait_sent(STEPS - 1)


def last_kernel(now2, now3, total, img_in, halo, cou, fwd, source,
                image_out, now_out, before_out, now4, img, sems):
    keep = pltpu.make_async_copy(now3, before_out, sems.at[0])
    keep.start()
    rest = (now2, now4, cou, fwd, img_in, img, (total, source.at[STEPS - 1]))
    copies = []

    def store(planes):
        for src, dst in ((now4, now_out), (img, image_out)):
            copies.append(pltpu.make_async_copy(src.at[planes], dst.at[planes], sems.at[1 + len(copies)]))
            copies[-1].start()

    for c in CHUNKS:
        outer(c, halo, now3, *rest)
    store(pl.ds(0, 4))
    store(pl.ds(CX - 4, 4))
    inner(now3, *rest)
    store(pl.ds(4, CX - 8))
    keep.wait()
    for copy in copies:
        copy.wait()


def local(courant, current, previous, image_in, forward_tt, traces, trace_owner, receiver_cell):
    dma = pltpu.SemaphoreType.DMA
    vmem, anywhere = pl.BlockSpec(memory_space=pltpu.VMEM), pl.BlockSpec(memory_space=pl.ANY)
    tile = pltpu.VMEM(TILE, F32)
    halo = pltpu.VMEM((2, 4, CY, CZ), F32)

    def kept(*arrays):
        return [pltpu.with_memory_space_constraint(a, pltpu.VMEM) for a in arrays]

    def far(*arrays):
        return [pltpu.with_memory_space_constraint(a, pltpu.HBM) for a in arrays]

    def edge_buffers(n):
        return [
            pltpu.VMEM((n, 2, 128, CZ), F32), pltpu.VMEM((n, 2, 128, CZ), F32),
            pltpu.VMEM((n, 2, CY, 128), F32), pltpu.VMEM((n, 2, CY, 128), F32),
        ]

    def edge_sems(n):
        return [dma((n, 4, 2)), dma((n, 4, 2)), dma((n, 2, 2)), dma((n, 2, 2)), dma((n, 2)), dma((n, 2))]

    outs = pl.pallas_call(
        first_kernel,
        out_shape=[
            tile, tile, tile, tile, tile, halo,
            pltpu.VMEM((CAP * STEPS, 128), F32), pltpu.VMEM((24, 128), I32),
            pltpu.VMEM((CZ, CZ), BF16), pltpu.VMEM((CY, 2 * CY), BF16), pltpu.VMEM((192, 192), BF16),
            pltpu.VMEM((64, 64), BF16), pltpu.VMEM((128, 128), BF16),
        ],
        in_specs=[anywhere] * 7,
        out_specs=[vmem] * 13,
        scratch_shapes=[
            pltpu.VMEM((STEPS, RECS), F32), pltpu.VMEM((1, RECS), I32), pltpu.VMEM((1, RECS), I32),
            pltpu.VMEM((16, 8, 128), F32), pltpu.VMEM((16, 8, 128), F32),
            pltpu.VMEM((8, 16, 128), F32), pltpu.VMEM((8, 16, 128), F32),
            *edge_buffers(1), dma((7,)), *edge_sems(1), dma((4,)),
        ],
        compiler_params=pltpu.CompilerParams(collective_id=0, has_side_effects=True, vmem_limit_bytes=8 * MIB),
    )(*far(current, previous, courant, image_in, traces.T, trace_owner.T, receiver_cell[None, :]))
    cur, prev, cou, img, total0, halo0, values, targets, *weights = outs

    source = pl.pallas_call(
        source_kernel,
        out_shape=pltpu.VMEM((STEPS,) + TILE, F32),
        in_specs=[vmem, anywhere],
        out_specs=vmem,
        scratch_shapes=[
            pltpu.VMEM((CX * 2 * CY, STEPS, 128), F32),
            pltpu.VMEM((128, CAP * STEPS, 128), F32),
            pltpu.SMEM((24, 128), I32),
            dma(()),
        ],
        compiler_params=pltpu.CompilerParams(vmem_limit_bytes=14 * MIB),
    )(*kept(values, targets))

    now2, now3, total, img, halo3, fwd3 = pl.pallas_call(
        step_kernel,
        out_shape=[tile, tile, tile, tile, halo, tile],
        in_specs=[vmem] * 4 + [anywhere] + [vmem] * 8,
        out_specs=[vmem] * 6,
        scratch_shapes=[
            pltpu.VMEM((STEPS - 1,) + TILE, F32), tile, pltpu.VMEM((2, 2, 4, CY, CZ), F32), *edge_buffers(STEPS - 1), dma((STEPS,)), *edge_sems(STEPS - 1),
        ],
        compiler_params=pltpu.CompilerParams(collective_id=1, has_side_effects=True, vmem_limit_bytes=16 * MIB),
    )(*kept(cur, prev, cou, img), *far(forward_tt), *kept(total0, halo0, source, *weights))

    whole = jax.ShapeDtypeStruct(TILE, F32)
    return pl.pallas_call(
        last_kernel,
        out_shape=(whole, whole, whole),
        in_specs=[vmem] * 8,
        out_specs=(anywhere,) * 3,
        scratch_shapes=[tile, tile, dma((8,))],
        compiler_params=pltpu.CompilerParams(vmem_limit_bytes=8 * MIB),
    )(*kept(now2, now3, total, img, halo3, cou, fwd3, source))


def solution(mesh):
    cells = P("gx", "gy", "gz")
    every = ("gx", "gy", "gz")
    return jax.shard_map(
        local,
        mesh=mesh,
        in_specs=(cells, cells, cells, cells, P(None, "gx", "gy", "gz"), P(every, None), P(every, None), P(every)),
        out_specs=(cells, cells, cells),
        check_vma=False,
    )
```

profile of v0, /device:TPU:3, one launch (start us, length us, event | category | flops | bytes accessed | tf_op | source)
XLA Modules:
  0.0 52.7 jit_solution(10860217173236254484)
XLA Ops:
  0.6 15.5 %shard_map.103 = (f32[32,64,256]{2,1,0:T(8,128)S(1)}, f32[32,64,256]{2,1,0:T(8,128)S(1)}, f32[32,64,256]{2,1,0:T(8,128)S(1)}, f32[32,64,256]{2,1,0:T(8,128)S(1)}...) custom-call(f32[32,64,256]{2,1,0:T(8,128)} %current.1, ...), custom_call_target="tpu_custom_call" | custom-call | tf_op jit(solution)/shard_map/pallas_call | solution.py:556
  16.2 4.4 %shard_map.104.source = f32[4,32,64,256]{3,2,1,0:T(8,128)S(1)} custom-call(f32[32,128]{1,0:T(8,128)S(1)} %get-tuple-element.28.values, s32[24,128]{1,0:T(8,128)S(1)} %get-tuple-element.29.targets), custom_call_target="tpu_custom_call" | custom-call | tf_op jit(solution)/shard_map/pallas_call | solution.py:576
  20.6 28.9 %shard_map.105 = (f32[32,64,256]{2,1,0:T(8,128)S(1)}, f32[32,64,256]{2,1,0:T(8,128)S(1)}, f32[32,64,256]{2,1,0:T(8,128)S(1)}, f32[32,64,256]{2,1,0:T(8,128)S(1)}...) custom-call(f32[32,64,256]{2,1,0:T(8,128)S(1)} %get-tuple-element.22.cur, ...), custom_call_target="tpu_custom_call" | custom-call | tf_op jit(solution)/shard_map/pallas_call | solution.py:590
  49.4 3.2 %shard_map.106 = (f32[32,64,256]{2,1,0:T(8,128)}, f32[32,64,256]{2,1,0:T(8,128)}, f32[32,64,256]{2,1,0:T(8,128)}) custom-call(f32[32,64,256]{2,1,0:T(8,128)S(1)} %get-tuple-element.35.now2, f32[32,64,256]{2,1,0:T(8,128)S(1)} %get-tuple-element.36.now3, f32[32,64,256]{2,1,0:T(8,128)S(1)} %get-tuple-element.37.total, ...), custom_call_target="tpu_custom_call" | custom-call | tf_op jit(solution)/shard_map/pallas_call | solution.py:602
where the time goes:
time: 52.8 us; the launch traced here: 52.7 us
  Pallas kernels  52 us (98%)
  between operations  0.66 us (1%)
    pallas_call x1, Pallas kernels, local(): pl.pallas_call(step_kernel, out_shape=[tile, tile, tile, tile, halo, tile...  28.9 us
    pallas_call x1, Pallas kernels, local(): pl.pallas_call(first_kernel, out_shape=[tile, tile, tile, tile, tile, hal...  15.5 us
    pallas_call x1, Pallas kernels, local(): pl.pallas_call(source_kernel, out_shape=pltpu.VMEM((STEPS,) + TILE, F32),...  4.4 us
    pallas_call x1, Pallas kernels, local(): pl.pallas_call(last_kernel, out_shape=(whole, whole, whole), in_specs=[vm...  3.22 us

commit v1 on v0

--- a/solution.py
+++ b/solution.py
@@ -44,6 +44,7 @@
 PARTS = ((0, 7), (1, 2, 3, 4, 5, 6))
 PAIRS = ((0, 1, 14, 15), tuple(range(2, 14)))
 Y_ROWS = ((0, 32), (32, 96))
+Z_ROWS = ((48, 16), (0, 48))
 TILE = (CX, CY, CZ)
 MIB = 1024 * 1024
 
@@ -76,6 +77,7 @@
     block_of_lane = iota((CY, 128), 1) // 4
     own_block = lax.rem(block_of_lane + 32 - at.gz, 32)
     inside = block_of_lane == 31 * (1 - at.gz)
+    last_lanes = iota((16, 128), 1) >= 96
     row8 = iota((8, CZ), 0)
     half = pl.ds(pl.multiple_of((1 - at.gz) * 128, 128), 128)
 
@@ -87,8 +89,9 @@
             device_id=(at.gx, at.gy + 1 if side == 0 else at.gy - 1, at.gz), device_id_type=MESH)
 
     def z_copy(n, part):
+        rows = pl.ds(*Z_ROWS[part])
         return pltpu.make_async_remote_copy(
-            src_ref=zs.at[n, part], dst_ref=zr.at[n, part],
+            src_ref=zs.at[n, rows], dst_ref=zr.at[n, rows],
             send_sem=zs_sem.at[n, part], recv_sem=zr_sem.at[n, part],
             device_id=(at.gx, at.gy, 1 - at.gz), device_id_type=MESH)
 
@@ -104,6 +107,26 @@
                 yr[n, 1] = jnp.zeros(yr.shape[2:], F32)
 
     def send(n, part, v):
+        edge = jnp.zeros((CY, 128), F32)
+        for i, x in enumerate(4 * g + j for g in PARTS[part] for j in range(4)):
+            moved = pltpu.roll(v[x, :, half], 4 * i + 4, 1)
+            edge = jnp.where(own_block == i, moved, edge)
+        hi, lo = split(edge)
+        sums = dot(hi, edge_z[...]) + dot(lo, edge_z[...])
+        if part == 0:
+            few = sums[0:16]
+            for q in range(1, 4):
+                few = few + pltpu.roll(sums[16 * q:16 * q + 16], 32 * q, 1)
+        else:
+            few = []
+            for q in range(3):
+                rest = pltpu.roll(sums[48:64], 96 - 32 * q, 1)
+                few.append(jnp.where(last_lanes, rest, sums[16 * q:16 * q + 16]))
+            few = jnp.concatenate(few, axis=0)
+        first, count = Z_ROWS[part]
+        zs[n, first:first + count, :] = few
+        z_copy(n, part).start()
+
         first, count = Y_ROWS[part]
         packed_rows = []
         for p in PAIRS[part]:
@@ -120,18 +143,11 @@
         pl.when(at.up)(lambda: y_copy(n, part, 0).start())
         pl.when(at.down)(lambda: y_copy(n, part, 1).start())
 
-        edge = jnp.zeros((CY, 128), F32)
-        for g in PARTS[part]:
-            for x in range(4 * g, 4 * g + 4):
-                moved = pltpu.roll(v[x, :, half], (4 * x + 4) % 128, 1)
-                edge = jnp.where(own_block == x, moved, edge)
-        hi, lo = split(edge)
-        zs[n, part] = dot(hi, edge_z[...]) + dot(lo, edge_z[...])
-        z_copy(n, part).start()
 
     def add(n, part, total):
         pl.when(at.down)(lambda: y_copy(n, part, 0).wait_recv())
         pl.when(at.up)(lambda: y_copy(n, part, 1).wait_recv())
+        z_copy(n, part).wait_recv()
         first, count = Y_ROWS[part]
         for i, p in enumerate(PAIRS[part]):
             top = yr[n, 0, first + i * 8:first + i * 8 + 8, :]
@@ -140,12 +156,19 @@
             total[2 * p + 1, 0:8, :] += jnp.where(row8 < 4, pltpu.roll(top, 4, 0), 0.0)
             total[2 * p, CY - 8:CY, :] += jnp.where(row8 < 4, 0.0, pltpu.roll(end, 4, 0))
             total[2 * p + 1, CY - 8:CY, :] += jnp.where(row8 < 4, 0.0, end)
-        z_copy(n, part).wait_recv()
-        got = zr[n, part]
-        for g in PARTS[part]:
-            for x in range(4 * g, 4 * g + 4):
-                moved = pltpu.roll(got, (128 - 4 * x) % 128, 1)
-                total[x, :, half] += jnp.where(inside, moved, 0.0)
+        first, count = Z_ROWS[part]
+        got = zr[n, first:first + count, :]
+        if part == 0:
+            got = jnp.concatenate([got] + [pltpu.roll(got, 128 - 32 * q, 1) for q in range(1, 4)], axis=0)
+        else:
+            rest = pltpu.roll(got[0:16], 32, 1)
+            for q in range(1, 3):
+                rest = jnp.where(iota((16, 128), 1) // 32 == q, pltpu.roll(got[16 * q:16 * q + 16], 32 + 32 * q, 1), rest)
+            got = jnp.concatenate([got, rest], axis=0)
+        got = pltpu.roll(got, 124 * (1 - at.gz), 1)
+        for i, x in enumerate(4 * g + j for g in PARTS[part] for j in range(4)):
+            moved = pltpu.roll(got, (128 - 4 * i) % 128, 1)
+            total[x, :, half] += jnp.where(inside, moved, 0.0)
 
     def wait_sent(slots):
         for n in range(slots):
@@ -154,18 +177,19 @@
                 pl.when(at.down)(lambda: y_copy(n, part, 1).wait_send())
                 z_copy(n, part).wait_send()
 
-    def bands(part, v_at, total):
+    def bands(part, v_at, total, first=0, end=None):
         def body(i, carry):
             g = pick_from(PARTS[part], i)
             v = v_at[pl.ds(4 * g, 4)].reshape(4 * CY, CZ)
             hi, lo = split(v)
             here = dot(hi, band_z[...]) + dot(lo, band_z[...]) + CENTRE * v
-            for p in range(4):
-                rows = slice(p * CY, (p + 1) * CY)
-                both = jnp.concatenate([hi[rows], lo[rows]], axis=0)
-                total[4 * g + p] = here[rows] + dot(band_y[...], both)
+            for p in (0, 2):
+                one, two = slice(p * CY, (p + 1) * CY), slice((p + 1) * CY, (p + 2) * CY)
+                both = jnp.concatenate([hi[one], lo[one], hi[two], lo[two]], axis=0)
+                sums = here[p * CY:(p + 2) * CY] + dot(band_y[...], both)
+                total[pl.ds(4 * g + p, 2)] = sums.reshape(2, CY, CZ)
             return carry
-        lax.fori_loop(0, len(PARTS[part]), body, 0)
+        lax.fori_loop(first, end or len(PARTS[part]), body, 0, unroll=2)
 
     return SimpleNamespace(clear=clear, send=send, add=add, wait_sent=wait_sent, bands=bands)
 
@@ -179,8 +203,8 @@
         device_id=(at.gx + 1 if side == 0 else at.gx - 1, at.gy, at.gz), device_id_type=MESH)
 
 
-def first_kernel(current, previous, courant, image_in, traces, owners, cells,
-                 cur, prev, cou, img, total, halo, values, targets,
+def first_kernel(current, previous, courant, image_in, forward, traces, owners, cells,
+                 cur, prev, cou, img, fwd0, total, halo, field_a, field_b, values, targets,
                  band_z, band_y, edge_y, edge_y_few, edge_z,
                  tr, ow, ce, packed, r1, t1, r2, ys, yr, zs, zr,
                  in_sem, xs_sem, xr_sem, ys_sem, yr_sem, zs_sem, zr_sem, route_sem):
@@ -194,8 +218,9 @@
         pltpu.make_async_copy(courant, cou, in_sem.at[4]),
         pltpu.make_async_copy(previous, prev, in_sem.at[5]),
         pltpu.make_async_copy(image_in, img, in_sem.at[6]),
+        pltpu.make_async_copy(forward.at[0], fwd0, in_sem.at[7]),
     ]
-    for load in loads:
+    for load in loads[:4]:
         load.start()
 
     barrier = pltpu.get_barrier_semaphore()
@@ -218,6 +243,16 @@
 
     lax.fori_loop(1, 16, greet_line, 0)
     lax.fori_loop(1, 8, greet_group, 0)
+
+    r_, c_ = iota((CZ, CZ), 0), iota((CZ, CZ), 1)
+    band_z[...] = tap_of(jnp.abs(r_ - c_)).astype(BF16)
+    r_, c_ = iota((2 * CY, 4 * CY), 0), iota((2 * CY, 4 * CY), 1)
+    gap = jnp.abs(lax.rem(r_, CY) - lax.rem(c_, CY))
+    band_y[...] = jnp.where(r_ // CY == c_ // (2 * CY), tap_of(gap), 0.0).astype(BF16)
+    edge_z[...] = edges(128, 31 * at.gz, at.gz == 0).astype(BF16)
+    for matrix, n in ((edge_y_few, 64), (edge_y, 192)):
+        upward = iota((n, n), 0) < n // 2
+        matrix[...] = edges(n, 0, ~upward).astype(BF16)
 
     for load in loads[:3]:
         load.wait()
@@ -267,15 +302,6 @@
         pl.when(at.left)(lambda: x_face(c, 1).start())
     r1[0] = packed[at.gx]
 
-    r_, c_ = iota((CZ, CZ), 0), iota((CZ, CZ), 1)
-    band_z[...] = tap_of(jnp.abs(r_ - c_)).astype(BF16)
-    r_, c_ = iota((CY, 2 * CY), 0), iota((CY, 2 * CY), 1)
-    band_y[...] = tap_of(jnp.abs(r_ - lax.rem(c_, CY))).astype(BF16)
-    edge_z[...] = edges(128, 30 * at.gz, at.gz == 0).astype(BF16)
-    for matrix, n in ((edge_y_few, 64), (edge_y, 192)):
-        upward = iota((n, n), 0) < n // 2
-        matrix[...] = edges(n, 0, ~upward).astype(BF16)
-
     face = faces(at, ys, yr, zs, zr, ys_sem, yr_sem, zs_sem, zr_sem,
                  (band_z, band_y, edge_y, edge_y_few, edge_z))
     face.clear(1)
@@ -283,8 +309,17 @@
     pl.when(~at.right)(lambda: halo.__setitem__(1, jnp.zeros(halo.shape[1:], F32)))
 
     loads[3].wait()
+    for load in loads[4:]:
+        load.start()
     face.send(0, 0, cur)
     face.send(0, 1, cur)
+    for field in (field_a, field_b):
+        rows = field.reshape(CX * 2 * CY * STEPS, 128)
+
+        def blank(i, carry):
+            rows[pl.ds(pl.multiple_of(i * 512, 512), 512), :] = jnp.zeros((512, 128), F32)
+            return carry
+        lax.fori_loop(0, CX * 2 * CY * STEPS // 512, blank, 0)
 
     pltpu.make_async_copy(r1.at[pl.ds(1, 15)], r1.at[pl.ds(1, 15)], route_sem.at[1]).wait()
     for j in range(8):
@@ -337,81 +372,69 @@
     face.wait_sent(1)
 
 
-def source_kernel(values, targets, source, field, spread, where, sem):
+def source_kernel(values, targets, blank_a, blank_b, field_a, field_b, spread, where, sem):
+    del blank_a, blank_b
     fetch = pltpu.make_async_copy(targets, where, sem)
     fetch.start()
-    rows = field.reshape(CX * 2 * CY * STEPS, 128)
-
-    def blank(i, carry):
-        rows[pl.ds(pl.multiple_of(i * 512, 512), 512), :] = jnp.zeros((512, 128), F32)
-        return carry
-    lax.fori_loop(0, CX * 2 * CY * STEPS // 512, blank, 0)
     for p in range(128):
         spread[p] = jnp.broadcast_to(values[:, p:p + 1], (CAP * STEPS, 128))
     fetch.wait()
     lanes = iota((STEPS, 128), 1)
 
-    def put(entries):
-        row = [where[r, p] for p, r in entries]
-        part = [jnp.where(lanes == where[CAP + r, p], spread[p, STEPS * r:STEPS * (r + 1), :], 0.0) for p, r in entries]
-        old = [field[i] for i in row]
-        for i in range(len(entries)):
-            total = old[i] + part[i]
-            for j in range(len(entries)):
-                if j != i:
-                    total = total + jnp.where(row[i] == row[j], part[j], 0.0)
-            old[i] = total
-        for i in range(len(entries)):
-            field[row[i]] = old[i]
-
-    def two(i, carry):
-        a, b = 2 * i, 2 * i + 1
-        put(((a, 0), (a, 1), (b, 0), (b, 1)))
-
-        @pl.when((where[2 * CAP, a] > 2) | (where[2 * CAP, b] > 2))
+    def put(p, r):
+        for field, n in ((field_a, r), (field_b, r + 1)):
+            row = where[n, p]
+            part = jnp.where(lanes == where[CAP + n, p], spread[p, STEPS * n:STEPS * (n + 1), :], 0.0)
+            field[row] = field[row] + part
+
+    def one(p, carry):
+        held = where[2 * CAP, p]
+        put(p, 0)
+
+        @pl.when(held > 2)
         def _():
-            put(((a, 2), (a, 3), (b, 2), (b, 3)))
-
-            @pl.when((where[2 * CAP, a] > 4) | (where[2 * CAP, b] > 4))
+            put(p, 2)
+
+            @pl.when(held > 4)
             def _():
-                put(((a, 4), (a, 5), (b, 4), (b, 5)))
-                put(((a, 6), (a, 7), (b, 6), (b, 7)))
-        return carry
-    lax.fori_loop(0, 64, two, 0)
-
-    def arrange(x, carry):
-        for k in range(STEPS):
-            for h in range(2):
-                for t in range(CY // 8):
-                    first = ((x * 2 + h) * CY + t * 8) * STEPS + k
-                    source[k, x, 8 * t:8 * t + 8, 128 * h:128 * h + 128] = rows[pl.ds(first, 8, stride=STEPS), :]
-        return carry
-    lax.fori_loop(0, CX, arrange, 0)
-
-
-def update(planes, rows, window, before, after, cou, fwd, image, image_after, totals):
+                put(p, 4)
+                put(p, 6)
+        return carry
+    lax.fori_loop(0, 128, one, 0)
+
+
+def source_at(fields, k, x, t):
+    halves = []
+    for h in range(2):
+        rows = pl.ds(((x * 2 + h) * CY + t * 8) * STEPS + k, 8, stride=STEPS)
+        halves.append(fields[0][rows, :] + fields[1][rows, :])
+    return jnp.concatenate(halves, axis=1)
+
+
+def update(k, planes, t, window, before, after, cou, fwd, image, image_after, total, fields):
+    rows = pl.ds(pl.multiple_of(t * 8, 8), 8)
     for x in planes:
         v = window(x)
-        total = totals[0][x, rows, :]
-        for more in totals[1:]:
-            total = total + more[x, rows, :]
+        here = total[x, rows, :]
+        if fields:
+            here = here + source_at(fields, k, x, t)
         for o in range(1, 5):
-            total = total + TAPS[o] * (window(x - o) + window(x + o))
-        new = (v + v) - before[x, rows, :] + cou[x, rows, :] * total
+            here = here + TAPS[o] * (window(x - o) + window(x + o))
+        new = (v + v) - before[x, rows, :] + cou[x, rows, :] * here
         after[x, rows, :] = new
         image_after[x, rows, :] = image[x, rows, :] + fwd[x, rows, :] * new
 
 
-def inner(v, *rest):
+def inner(k, v, *rest):
     def body(t, carry):
         rows = pl.ds(pl.multiple_of(t * 8, 8), 8)
         planes = {x: v[x, rows, :] for x in range(CX)}
-        update(range(4, CX - 4), rows, lambda x: planes[x], *rest)
+        update(k, range(4, CX - 4), t, lambda x: planes[x], *rest)
         return carry
     lax.fori_loop(0, CY // 8, body, 0)
 
 
-def outer(c, halo, v, *rest):
+def outer(k, c, halo, v, *rest):
     def body(t, carry):
         rows = pl.ds(pl.multiple_of(t * 8, 8), 8)
         for side in range(2):
@@ -420,17 +443,23 @@
             for i in range(4):
                 planes[i - 4 if side == 0 else CX + i] = halo[side, i, rows, :]
             here = range(0, 4) if side == 0 else range(CX - 4, CX)
-            update(here, rows, lambda x: planes[x], *rest)
+            update(k, here, t, lambda x: planes[x], *rest)
         return carry
     lax.fori_loop(c * ROWS // 8, (c + 1) * ROWS // 8, body, 0)
 
 
-def step_kernel(cur, prev, cou, img_in, forward, total0, halo0, source, band_z, band_y, edge_y, edge_y_few, edge_z,
-                now2, now3, total, img, halo3, fwd3,
+def flat(*fields):
+    return [field.reshape(CX * 2 * CY * STEPS, 128) for field in fields]
+
+
+def step_kernel(cur, prev, cou, img_in, forward, fwd0, total0, halo0, field_a, field_b,
+                band_z, band_y, edge_y, edge_y_few, edge_z,
+                now2, now3, now4, total, img, halo3,
                 fwd, now1, halos, ys, yr, zs, zr,
                 in_sem, xs_sem, xr_sem, ys_sem, yr_sem, zs_sem, zr_sem):
     at = place()
-    loads = [pltpu.make_async_copy(forward.at[k], fwd3 if k == STEPS - 1 else fwd.at[k], in_sem.at[k]) for k in range(STEPS)]
+    fwd_at = [fwd0, fwd.at[0], fwd.at[1], fwd.at[2]]
+    loads = [pltpu.make_async_copy(forward.at[k], fwd_at[k], in_sem.at[k]) for k in range(1, STEPS)]
     for load in loads:
         load.start()
     barrier = pltpu.get_barrier_semaphore()
@@ -446,14 +475,15 @@
     one = lambda yes: jnp.where(yes, 1, 0)
     neighbours = 1 + one(at.right) + one(at.left) + one(at.up) + one(at.down)
 
-    v_at = [prev, cur, now1, now2, now3]
+    v_at = [prev, cur, now1, now2, now3, now4]
     halo = [halo0, halos.at[0], halos.at[1], halo3]
+    fields = flat(field_a, field_b)
     face = faces(at, ys, yr, zs, zr, ys_sem, yr_sem, zs_sem, zr_sem,
                  (band_z, band_y, edge_y, edge_y_few, edge_z))
 
     def rest(k):
-        totals = (total0, source.at[0]) if k == 0 else (total, source.at[k])
-        return (v_at[k], v_at[k + 2], cou, fwd.at[k], img_in if k == 0 else img, img, totals)
+        first = k == 0
+        return (v_at[k], v_at[k + 2], cou, fwd_at[k], img_in if first else img, img, total0 if first else total, fields)
 
     def x_face(k, c, side):
         return x_copy(at, v_at[k + 1], halo[k], (xs_sem, xr_sem), k - 1, c, side)
@@ -471,35 +501,38 @@
         pl.when(~at.left)(lambda: halo[k].__setitem__(0, jnp.zeros(halo3.shape[1:], F32)))
         pl.when(~at.right)(lambda: halo[k].__setitem__(1, jnp.zeros(halo3.shape[1:], F32)))
 
-    loads[0].wait()
+    def last_sources():
+        def body(t, carry):
+            rows = pl.ds(pl.multiple_of(t * 8, 8), 8)
+            for x in (0, 1, 2, 3, CX - 4, CX - 3, CX - 2, CX - 1):
+                total[x, rows, :] += source_at(fields, STEPS - 1, x, t)
+            return carry
+        lax.fori_loop(0, CY // 8, body, 0)
+
     for c in CHUNKS:
-        outer(c, halo0, cur, *rest(0))
+        outer(0, c, halo0, cur, *rest(0))
     pl.semaphore_wait(barrier, neighbours)
     for c in CHUNKS:
         x_start(1, c)
     face.send(0, 0, now1)
-    inner(cur, *rest(0))
-    for k in range(1, STEPS - 1):
+    inner(0, cur, *rest(0))
+    for k in range(1, STEPS):
         v = v_at[k + 1]
         face.send(k - 1, 1, v)
         face.bands(0, v, total)
+        face.bands(1, v, total)
         face.add(k - 1, 0, total)
-        loads[k].wait()
-        for c in CHUNKS:
-            x_wait(k, c)
-            outer(c, halo[k], v, *rest(k))
-            x_start(k + 1, c)
-        face.send(k, 0, v_at[k + 2])
-        face.bands(1, v, total)
+        loads[k - 1].wait()
+        if k < STEPS - 1:
+            for c in CHUNKS:
+                x_wait(k, c)
+                outer(k, c, halo[k], v, *rest(k))
+                x_start(k + 1, c)
+            face.send(k, 0, v_at[k + 2])
+        else:
+            last_sources()
         face.add(k - 1, 1, total)
-        inner(v, *rest(k))
-    last = STEPS - 2
-    face.send(last, 1, now3)
-    face.bands(0, now3, total)
-    face.bands(1, now3, total)
-    face.add(last, 0, total)
-    face.add(last, 1, total)
-    loads[STEPS - 1].wait()
+        inner(k, v, *rest(k))
     for c in CHUNKS:
         x_wait(STEPS - 1, c)
     for k in range(1, STEPS):
@@ -509,25 +542,28 @@
     face.wait_sent(STEPS - 1)
 
 
-def last_kernel(now2, now3, total, img_in, halo, cou, fwd, source,
-                image_out, now_out, before_out, now4, img, sems):
-    keep = pltpu.make_async_copy(now3, before_out, sems.at[0])
-    keep.start()
-    rest = (now2, now4, cou, fwd, img_in, img, (total, source.at[STEPS - 1]))
+def last_kernel(now2, now3, now4_in, total, img_in, halo, cou, forward,
+                image_out, now_out, before_out, fwd, now4, img, sems, in_sem):
     copies = []
-
-    def store(planes):
-        for src, dst in ((now4, now_out), (img, image_out)):
-            copies.append(pltpu.make_async_copy(src.at[planes], dst.at[planes], sems.at[1 + len(copies)]))
-            copies[-1].start()
-
+    sides = (pl.ds(0, 4), pl.ds(CX - 4, 4))
+    loads = [pltpu.make_async_copy(forward.at[STEPS - 1, planes], fwd.at[planes], in_sem.at[i]) for i, planes in enumerate(sides)]
+    for load in loads:
+        load.start()
+
+    def store(src, dst, planes):
+        copies.append(pltpu.make_async_copy(src.at[planes], dst.at[planes], sems.at[len(copies)]))
+        copies[-1].start()
+
+    store(now4_in, now_out, pl.ds(4, CX - 8))
+    store(img_in, image_out, pl.ds(4, CX - 8))
+    store(now3, before_out, pl.ds(0, CX))
+    for load in loads:
+        load.wait()
     for c in CHUNKS:
-        outer(c, halo, now3, *rest)
-    store(pl.ds(0, 4))
-    store(pl.ds(CX - 4, 4))
-    inner(now3, *rest)
-    store(pl.ds(4, CX - 8))
-    keep.wait()
+        outer(STEPS - 1, c, halo, now3, now2, now4, cou, fwd, img_in, img, total, None)
+    for planes in sides:
+        store(now4, now_out, planes)
+        store(img, image_out, planes)
     for copy in copies:
         copy.wait()
 
@@ -537,6 +573,7 @@
     vmem, anywhere = pl.BlockSpec(memory_space=pltpu.VMEM), pl.BlockSpec(memory_space=pl.ANY)
     tile = pltpu.VMEM(TILE, F32)
     halo = pltpu.VMEM((2, 4, CY, CZ), F32)
+    field = pltpu.VMEM((CX * 2 * CY, STEPS, 128), F32)
 
     def kept(*arrays):
         return [pltpu.with_memory_space_constraint(a, pltpu.VMEM) for a in arrays]
@@ -547,7 +584,7 @@
     def edge_buffers(n):
         return [
             pltpu.VMEM((n, 2, 128, CZ), F32), pltpu.VMEM((n, 2, 128, CZ), F32),
-            pltpu.VMEM((n, 2, CY, 128), F32), pltpu.VMEM((n, 2, CY, 128), F32),
+            pltpu.VMEM((n, CY, 128), F32), pltpu.VMEM((n, CY, 128), F32),
         ]
 
     def edge_sems(n):
@@ -556,57 +593,59 @@
     outs = pl.pallas_call(
         first_kernel,
         out_shape=[
-            tile, tile, tile, tile, tile, halo,
+            tile, tile, tile, tile, tile, tile, halo,
+            field, field,
             pltpu.VMEM((CAP * STEPS, 128), F32), pltpu.VMEM((24, 128), I32),
-            pltpu.VMEM((CZ, CZ), BF16), pltpu.VMEM((CY, 2 * CY), BF16), pltpu.VMEM((192, 192), BF16),
+            pltpu.VMEM((CZ, CZ), BF16), pltpu.VMEM((2 * CY, 4 * CY), BF16), pltpu.VMEM((192, 192), BF16),
             pltpu.VMEM((64, 64), BF16), pltpu.VMEM((128, 128), BF16),
         ],
-        in_specs=[anywhere] * 7,
-        out_specs=[vmem] * 13,
+        in_specs=[anywhere] * 8,
+        out_specs=[vmem] * 16,
         scratch_shapes=[
             pltpu.VMEM((STEPS, RECS), F32), pltpu.VMEM((1, RECS), I32), pltpu.VMEM((1, RECS), I32),
             pltpu.VMEM((16, 8, 128), F32), pltpu.VMEM((16, 8, 128), F32),
             pltpu.VMEM((8, 16, 128), F32), pltpu.VMEM((8, 16, 128), F32),
-            *edge_buffers(1), dma((7,)), *edge_sems(1), dma((4,)),
+            *edge_buffers(1), dma((8,)), *edge_sems(1), dma((4,)),
         ],
         compiler_params=pltpu.CompilerParams(collective_id=0, has_side_effects=True, vmem_limit_bytes=8 * MIB),
-    )(*far(current, previous, courant, image_in, traces.T, trace_owner.T, receiver_cell[None, :]))
-    cur, prev, cou, img, total0, halo0, values, targets, *weights = outs
-
-    source = pl.pallas_call(
+    )(*far(current, previous, courant, image_in, forward_tt, traces.T, trace_owner.T, receiver_cell[None, :]))
+    cur, prev, cou, img, fwd0, total0, halo0, field_a, field_b, values, targets, *weights = outs
+
+    fields = pl.pallas_call(
         source_kernel,
-        out_shape=pltpu.VMEM((STEPS,) + TILE, F32),
-        in_specs=[vmem, anywhere],
-        out_specs=vmem,
+        out_shape=[field, field],
+        in_specs=[vmem, anywhere, vmem, vmem],
+        out_specs=[vmem, vmem],
+        input_output_aliases={2: 0, 3: 1},
         scratch_shapes=[
-            pltpu.VMEM((CX * 2 * CY, STEPS, 128), F32),
             pltpu.VMEM((128, CAP * STEPS, 128), F32),
             pltpu.SMEM((24, 128), I32),
             dma(()),
         ],
-        compiler_params=pltpu.CompilerParams(vmem_limit_bytes=14 * MIB),
-    )(*kept(values, targets))
-
-    now2, now3, total, img, halo3, fwd3 = pl.pallas_call(
+        compiler_params=pltpu.CompilerParams(vmem_limit_bytes=4 * MIB),
+    )(*kept(values, targets, field_a, field_b))
+
+    now2, now3, now4, total, img, halo3 = pl.pallas_call(
         step_kernel,
-        out_shape=[tile, tile, tile, tile, halo, tile],
-        in_specs=[vmem] * 4 + [anywhere] + [vmem] * 8,
+        out_shape=[tile, tile, tile, tile, tile, halo],
+        in_specs=[vmem] * 4 + [anywhere] + [vmem] * 10,
         out_specs=[vmem] * 6,
         scratch_shapes=[
-            pltpu.VMEM((STEPS - 1,) + TILE, F32), tile, pltpu.VMEM((2, 2, 4, CY, CZ), F32), *edge_buffers(STEPS - 1), dma((STEPS,)), *edge_sems(STEPS - 1),
+            pltpu.VMEM((STEPS - 1,) + TILE, F32), tile, pltpu.VMEM((2, 2, 4, CY, CZ), F32),
+            *edge_buffers(STEPS - 1), dma((STEPS,)), *edge_sems(STEPS - 1),
         ],
-        compiler_params=pltpu.CompilerParams(collective_id=1, has_side_effects=True, vmem_limit_bytes=16 * MIB),
-    )(*kept(cur, prev, cou, img), *far(forward_tt), *kept(total0, halo0, source, *weights))
+        compiler_params=pltpu.CompilerParams(collective_id=1, has_side_effects=True, vmem_limit_bytes=13 * MIB),
+    )(*kept(cur, prev, cou, img), *far(forward_tt), *kept(fwd0, total0, halo0, *fields, *weights))
 
     whole = jax.ShapeDtypeStruct(TILE, F32)
     return pl.pallas_call(
         last_kernel,
         out_shape=(whole, whole, whole),
-        in_specs=[vmem] * 8,
+        in_specs=[vmem] * 7 + [anywhere],
         out_specs=(anywhere,) * 3,
-        scratch_shapes=[tile, tile, dma((8,))],
+        scratch_shapes=[tile, tile, tile, dma((8,)), dma((2,))],
         compiler_params=pltpu.CompilerParams(vmem_limit_bytes=8 * MIB),
-    )(*kept(now2, now3, total, img, halo3, cou, fwd3, source))
+    )(*kept(now2, now3, now4, total, img, halo3, cou), *far(forward_tt))
 
 
 def solution(mesh):

time: 52.8 us -> 49 us (0.928)
  Pallas kernels: 52 us -> 48.2 us
    pallas_call x3, Pallas kernels: 48.8 us -> 45.4 us  [the longest x1 26.8 us: local(): pl.pallas_call(step_kernel, out_shape=[tile, tile, tile, tile, tile, halo...]
where the time goes in v1:
time: 49 us; the launch traced here: 48.8 us
  Pallas kernels  48.2 us (98%)
  between operations  0.66 us (1%)
    pallas_call x1, Pallas kernels, local(): pl.pallas_call(step_kernel, out_shape=[tile, tile, tile, tile, tile, halo...  26.8 us
    pallas_call x1, Pallas kernels, local(): pl.pallas_call(first_kernel, out_shape=[tile, tile, tile, tile, tile, til...  15.6 us
    pallas_call x1, Pallas kernels, local(): pl.pallas_call(source_kernel, out_shape=[field, field], in_specs=[vmem, a...  3.05 us
    pallas_call x1, Pallas kernels, local(): pl.pallas_call(last_kernel, out_shape=(whole, whole, whole), in_specs=[vm...  2.8 us

profile of v1, /device:TPU:3, one launch (start us, length us, event | category | flops | bytes accessed | tf_op | source)
XLA Modules:
  0.0 48.8 jit_solution(10197011423863319705)
XLA Ops:
  0.6 15.6 %shard_map.103 = (f32[32,64,256]{2,1,0:T(8,128)S(1)}, f32[32,64,256]{2,1,0:T(8,128)S(1)}, f32[32,64,256]{2,1,0:T(8,128)S(1)}, f32[32,64,256]{2,1,0:T(8,128)S(1)}...) custom-call(f32[32,64,256]{2,1,0:T(8,128)} %current.1, ...), custom_call_target="tpu_custom_call" | custom-call | tf_op jit(solution)/shard_map/pallas_call | solution.py:593
  16.2 3.1 %shard_map.104 = (f32[4096,4,128]{2,1,0:T(4,128)S(1)}, f32[4096,4,128]{2,1,0:T(4,128)S(1)}) custom-call(f32[32,128]{1,0:T(8,128)S(1)} %get-tuple-element.34.values, s32[24,128]{1,0:T(8,128)S(1)} %get-tuple-element.35.targets, f32[4096,4,128]{2,1,0:T(4,128)S(1)} %get-tuple-element.36.blank_a, ...), custom_call_target="tpu_custom_call", output_to_operand_aliasing={{0}: (2, {}), {1}: (3, {})} | custom-call | tf_op jit(solution)/shard_map/pallas_call | solution.py:614
  19.3 26.8 %shard_map.105 = (f32[32,64,256]{2,1,0:T(8,128)S(1)}, f32[32,64,256]{2,1,0:T(8,128)S(1)}, f32[32,64,256]{2,1,0:T(8,128)S(1)}, f32[32,64,256]{2,1,0:T(8,128)S(1)}...) custom-call(f32[32,64,256]{2,1,0:T(8,128)S(1)} %get-tuple-element.27.cur, ...), custom_call_target="tpu_custom_call" | custom-call | tf_op jit(solution)/shard_map/pallas_call | solution.py:628
  46.0 2.8 %shard_map.106 = (f32[32,64,256]{2,1,0:T(8,128)}, f32[32,64,256]{2,1,0:T(8,128)}, f32[32,64,256]{2,1,0:T(8,128)}) custom-call(f32[32,64,256]{2,1,0:T(8,128)S(1)} %get-tuple-element.45.now2, f32[32,64,256]{2,1,0:T(8,128)S(1)} %get-tuple-element.46.now3, f32[32,64,256]{2,1,0:T(8,128)S(1)} %get-tuple-element.47.now4_in, ...), custom_call_target="tpu_custom_call" | custom-call | tf_op jit(solution)/shard_map/pallas_call | solution.py:641

commit v2 on v1

--- a/solution.py
+++ b/solution.py
@@ -13,7 +13,7 @@
 N_GX, N_GY, N_GZ = 16, 4, 2
 RECS = 256
 ROWS = 16
-CHUNKS = (1, 2, 0, 3)
+CHUNKS = (0, 3, 1, 2)
 SCALE = 5040.0
 TAPS = (0.0, 8064.0, -1008.0, 128.0, -9.0)
 CENTRE = -43050.0
@@ -44,7 +44,8 @@
 PARTS = ((0, 7), (1, 2, 3, 4, 5, 6))
 PAIRS = ((0, 1, 14, 15), tuple(range(2, 14)))
 Y_ROWS = ((0, 32), (32, 96))
-Z_ROWS = ((48, 16), (0, 48))
+Z_ROWS = ((48, 32), (0, 48), (80, 32))
+SPANS = {0: ((0, 16), (48, 16)), 2: ((16, 32),)}
 TILE = (CX, CY, CZ)
 MIB = 1024 * 1024
 
@@ -107,25 +108,25 @@
                 yr[n, 1] = jnp.zeros(yr.shape[2:], F32)
 
     def send(n, part, v):
-        edge = jnp.zeros((CY, 128), F32)
-        for i, x in enumerate(4 * g + j for g in PARTS[part] for j in range(4)):
-            moved = pltpu.roll(v[x, :, half], 4 * i + 4, 1)
-            edge = jnp.where(own_block == i, moved, edge)
+        if part == 1:
+            edge = jnp.zeros((CY, 128), F32)
+            for i, x in enumerate(range(4, CX - 4)):
+                edge = jnp.where(own_block == i, pltpu.roll(v[x, :, half], 4 * i + 4, 1), edge)
+        else:
+            edge = jnp.zeros((32, 128), F32)
+            for i, x in enumerate((0, 1, 2, 3, CX - 4, CX - 3, CX - 2, CX - 1)):
+                rows = jnp.concatenate([v[x, at_row:at_row + rows, half] for at_row, rows in SPANS[part]], axis=0)
+                edge = jnp.where(own_block[0:32] == i, pltpu.roll(rows, 4 * i + 4, 1), edge)
         hi, lo = split(edge)
-        sums = dot(hi, edge_z[...]) + dot(lo, edge_z[...])
-        if part == 0:
-            few = sums[0:16]
-            for q in range(1, 4):
-                few = few + pltpu.roll(sums[16 * q:16 * q + 16], 32 * q, 1)
-        else:
-            few = []
-            for q in range(3):
-                rest = pltpu.roll(sums[48:64], 96 - 32 * q, 1)
-                few.append(jnp.where(last_lanes, rest, sums[16 * q:16 * q + 16]))
-            few = jnp.concatenate(few, axis=0)
+        few = dot(hi, edge_z[...]) + dot(lo, edge_z[...])
+        if part == 1:
+            moved = [pltpu.roll(few[48:64], 96 - 32 * q, 1) for q in range(3)]
+            few = jnp.concatenate([jnp.where(last_lanes, moved[q], few[16 * q:16 * q + 16]) for q in range(3)], axis=0)
         first, count = Z_ROWS[part]
         zs[n, first:first + count, :] = few
         z_copy(n, part).start()
+        if part == 2:
+            return
 
         first, count = Y_ROWS[part]
         packed_rows = []
@@ -145,9 +146,27 @@
 
 
     def add(n, part, total):
+        z_copy(n, part).wait_recv()
+        first, count = Z_ROWS[part]
+        got = zr[n, first:first + count, :]
+        if part == 1:
+            rest = pltpu.roll(got[0:16], 32, 1)
+            for q in range(1, 3):
+                rest = jnp.where(iota((16, 128), 1) // 32 == q, pltpu.roll(got[16 * q:16 * q + 16], 32 + 32 * q, 1), rest)
+            got = jnp.concatenate([got, rest], axis=0)
+        got = pltpu.roll(got, 124 * (1 - at.gz), 1)
+        for i, x in enumerate(4 * g + j for g in PARTS[part % 2] for j in range(4)):
+            moved = pltpu.roll(got, (128 - 4 * i) % 128, 1)
+            moved = jnp.where(inside[0:moved.shape[0]], moved, 0.0)
+            done = 0
+            for at_row, rows in SPANS.get(part, ((0, CY),)):
+                total[x, at_row:at_row + rows, half] += moved[done:done + rows]
+                done += rows
+        if part == 2:
+            return
+
         pl.when(at.down)(lambda: y_copy(n, part, 0).wait_recv())
         pl.when(at.up)(lambda: y_copy(n, part, 1).wait_recv())
-        z_copy(n, part).wait_recv()
         first, count = Y_ROWS[part]
         for i, p in enumerate(PAIRS[part]):
             top = yr[n, 0, first + i * 8:first + i * 8 + 8, :]
@@ -156,25 +175,13 @@
             total[2 * p + 1, 0:8, :] += jnp.where(row8 < 4, pltpu.roll(top, 4, 0), 0.0)
             total[2 * p, CY - 8:CY, :] += jnp.where(row8 < 4, 0.0, pltpu.roll(end, 4, 0))
             total[2 * p + 1, CY - 8:CY, :] += jnp.where(row8 < 4, 0.0, end)
-        first, count = Z_ROWS[part]
-        got = zr[n, first:first + count, :]
-        if part == 0:
-            got = jnp.concatenate([got] + [pltpu.roll(got, 128 - 32 * q, 1) for q in range(1, 4)], axis=0)
-        else:
-            rest = pltpu.roll(got[0:16], 32, 1)
-            for q in range(1, 3):
-                rest = jnp.where(iota((16, 128), 1) // 32 == q, pltpu.roll(got[16 * q:16 * q + 16], 32 + 32 * q, 1), rest)
-            got = jnp.concatenate([got, rest], axis=0)
-        got = pltpu.roll(got, 124 * (1 - at.gz), 1)
-        for i, x in enumerate(4 * g + j for g in PARTS[part] for j in range(4)):
-            moved = pltpu.roll(got, (128 - 4 * i) % 128, 1)
-            total[x, :, half] += jnp.where(inside, moved, 0.0)
 
     def wait_sent(slots):
         for n in range(slots):
             for part in range(2):
                 pl.when(at.up)(lambda: y_copy(n, part, 0).wait_send())
                 pl.when(at.down)(lambda: y_copy(n, part, 1).wait_send())
+            for part in range(3):
                 z_copy(n, part).wait_send()
 
     def bands(part, v_at, total, first=0, end=None):
@@ -312,6 +319,7 @@
     for load in loads[4:]:
         load.start()
     face.send(0, 0, cur)
+    face.send(0, 2, cur)
     face.send(0, 1, cur)
     for field in (field_a, field_b):
         rows = field.reshape(CX * 2 * CY * STEPS, 128)
@@ -344,6 +352,7 @@
         return carry
     lax.fori_loop(0, CX, rescale, 0)
     face.add(0, 0, total)
+    face.add(0, 2, total)
     face.add(0, 1, total)
 
     pltpu.make_async_copy(r2.at[pl.ds(1, 7)], r2.at[pl.ds(1, 7)], route_sem.at[3]).wait()
@@ -496,11 +505,6 @@
         pl.when(at.left)(lambda: x_face(k, c, 0).wait_recv())
         pl.when(at.right)(lambda: x_face(k, c, 1).wait_recv())
 
-    face.clear(STEPS - 1)
-    for k in range(1, STEPS):
-        pl.when(~at.left)(lambda: halo[k].__setitem__(0, jnp.zeros(halo3.shape[1:], F32)))
-        pl.when(~at.right)(lambda: halo[k].__setitem__(1, jnp.zeros(halo3.shape[1:], F32)))
-
     def last_sources():
         def body(t, carry):
             rows = pl.ds(pl.multiple_of(t * 8, 8), 8)
@@ -509,30 +513,50 @@
             return carry
         lax.fori_loop(0, CY // 8, body, 0)
 
+    pl.semaphore_wait(barrier, neighbours)
     for c in CHUNKS:
         outer(0, c, halo0, cur, *rest(0))
-    pl.semaphore_wait(barrier, neighbours)
-    for c in CHUNKS:
         x_start(1, c)
+    face.clear(STEPS - 1)
+    for k in range(1, STEPS):
+        pl.when(~at.left)(lambda: halo[k].__setitem__(0, jnp.zeros(halo3.shape[1:], F32)))
+        pl.when(~at.right)(lambda: halo[k].__setitem__(1, jnp.zeros(halo3.shape[1:], F32)))
+
     face.send(0, 0, now1)
+    face.send(0, 2, now1)
     inner(0, cur, *rest(0))
-    for k in range(1, STEPS):
-        v = v_at[k + 1]
+    for k in range(1, STEPS - 1):
+        v, then = v_at[k + 1], v_at[k + 2]
+
+        def chunk(c):
+            x_wait(k, c)
+            outer(k, c, halo[k], v, *rest(k))
+            x_start(k + 1, c)
+
         face.send(k - 1, 1, v)
         face.bands(0, v, total)
-        face.bands(1, v, total)
+        loads[k - 1].wait()
         face.add(k - 1, 0, total)
-        loads[k - 1].wait()
-        if k < STEPS - 1:
-            for c in CHUNKS:
-                x_wait(k, c)
-                outer(k, c, halo[k], v, *rest(k))
-                x_start(k + 1, c)
-            face.send(k, 0, v_at[k + 2])
-        else:
-            last_sources()
+        chunk(CHUNKS[0])
+        face.bands(1, v, total, 0, 4)
+        chunk(CHUNKS[1])
+        face.send(k, 0, then)
+        face.bands(1, v, total, 4, 6)
+        face.add(k - 1, 2, total)
+        chunk(CHUNKS[2])
         face.add(k - 1, 1, total)
         inner(k, v, *rest(k))
+        chunk(CHUNKS[3])
+        face.send(k, 2, then)
+    last = STEPS - 2
+    face.send(last, 1, now3)
+    face.bands(0, now3, total)
+    face.bands(1, now3, total)
+    loads[last].wait()
+    for part in (0, 2, 1):
+        face.add(last, part, total)
+    last_sources()
+    inner(STEPS - 1, now3, *rest(STEPS - 1))
     for c in CHUNKS:
         x_wait(STEPS - 1, c)
     for k in range(1, STEPS):
@@ -584,11 +608,11 @@
     def edge_buffers(n):
         return [
             pltpu.VMEM((n, 2, 128, CZ), F32), pltpu.VMEM((n, 2, 128, CZ), F32),
-            pltpu.VMEM((n, CY, 128), F32), pltpu.VMEM((n, CY, 128), F32),
+            pltpu.VMEM((n, 112, 128), F32), pltpu.VMEM((n, 112, 128), F32),
         ]
 
     def edge_sems(n):
-        return [dma((n, 4, 2)), dma((n, 4, 2)), dma((n, 2, 2)), dma((n, 2, 2)), dma((n, 2)), dma((n, 2))]
+        return [dma((n, 4, 2)), dma((n, 4, 2)), dma((n, 2, 2)), dma((n, 2, 2)), dma((n, 3)), dma((n, 3))]
 
     outs = pl.pallas_call(
         first_kernel,

time: 49 us -> 48.6 us (level)
  Pallas kernels: 48.2 us -> 47.4 us
    pallas_call x1, Pallas kernels: 26.8 us -> 25.9 us  [local(): pl.pallas_call(step_kernel, out_shape=[tile, tile, tile, tile, tile, halo...]
where the time goes in v2:
time: 48.6 us; the launch traced here: 48 us
  Pallas kernels  47.4 us (98%)
  between operations  0.66 us (1%)
    pallas_call x1, Pallas kernels, local(): pl.pallas_call(step_kernel, out_shape=[tile, tile, tile, tile, tile, halo...  25.9 us
    pallas_call x1, Pallas kernels, local(): pl.pallas_call(first_kernel, out_shape=[tile, tile, tile, tile, tile, til...  15.6 us
    pallas_call x1, Pallas kernels, local(): pl.pallas_call(source_kernel, out_shape=[field, field], in_specs=[vmem, a...  3.06 us
    pallas_call x1, Pallas kernels, local(): pl.pallas_call(last_kernel, out_shape=(whole, whole, whole), in_specs=[vm...  2.8 us

profile of v2, /device:TPU:3, one launch (start us, length us, event | category | flops | bytes accessed | tf_op | source)
XLA Modules:
  0.0 48.0 jit_solution(11306166847792487011)
XLA Ops:
  0.6 15.6 %shard_map.103 = (f32[32,64,256]{2,1,0:T(8,128)S(1)}, f32[32,64,256]{2,1,0:T(8,128)S(1)}, f32[32,64,256]{2,1,0:T(8,128)S(1)}, f32[32,64,256]{2,1,0:T(8,128)S(1)}...) custom-call(f32[32,64,256]{2,1,0:T(8,128)} %current.1, ...), custom_call_target="tpu_custom_call" | custom-call | tf_op jit(solution)/shard_map/pallas_call | solution.py:617
  16.2 3.1 %shard_map.104 = (f32[4096,4,128]{2,1,0:T(4,128)S(1)}, f32[4096,4,128]{2,1,0:T(4,128)S(1)}) custom-call(f32[32,128]{1,0:T(8,128)S(1)} %get-tuple-element.34.values, s32[24,128]{1,0:T(8,128)S(1)} %get-tuple-element.35.targets, f32[4096,4,128]{2,1,0:T(4,128)S(1)} %get-tuple-element.36.blank_a, ...), custom_call_target="tpu_custom_call", output_to_operand_aliasing={{0}: (2, {}), {1}: (3, {})} | custom-call | tf_op jit(solution)/shard_map/pallas_call | solution.py:638
  19.3 25.9 %shard_map.105 = (f32[32,64,256]{2,1,0:T(8,128)S(1)}, f32[32,64,256]{2,1,0:T(8,128)S(1)}, f32[32,64,256]{2,1,0:T(8,128)S(1)}, f32[32,64,256]{2,1,0:T(8,128)S(1)}...) custom-call(f32[32,64,256]{2,1,0:T(8,128)S(1)} %get-tuple-element.27.cur, ...), custom_call_target="tpu_custom_call" | custom-call | tf_op jit(solution)/shard_map/pallas_call | solution.py:652
  45.2 2.8 %shard_map.106 = (f32[32,64,256]{2,1,0:T(8,128)}, f32[32,64,256]{2,1,0:T(8,128)}, f32[32,64,256]{2,1,0:T(8,128)}) custom-call(f32[32,64,256]{2,1,0:T(8,128)S(1)} %get-tuple-element.45.now2, f32[32,64,256]{2,1,0:T(8,128)S(1)} %get-tuple-element.46.now3, f32[32,64,256]{2,1,0:T(8,128)S(1)} %get-tuple-element.47.now4_in, ...), custom_call_target="tpu_custom_call" | custom-call | tf_op jit(solution)/shard_map/pallas_call | solution.py:665

commit v3 on v2

--- a/solution.py
+++ b/solution.py
@@ -396,20 +396,24 @@
             part = jnp.where(lanes == where[CAP + n, p], spread[p, STEPS * n:STEPS * (n + 1), :], 0.0)
             field[row] = field[row] + part
 
-    def one(p, carry):
-        held = where[2 * CAP, p]
-        put(p, 0)
+    def two(i, carry):
+        pair = (2 * i, 2 * i + 1)
+        held = jnp.maximum(where[2 * CAP, pair[0]], where[2 * CAP, pair[1]])
+        for p in pair:
+            put(p, 0)
 
         @pl.when(held > 2)
         def _():
-            put(p, 2)
+            for p in pair:
+                put(p, 2)
 
             @pl.when(held > 4)
             def _():
-                put(p, 4)
-                put(p, 6)
-        return carry
-    lax.fori_loop(0, 128, one, 0)
+                for p in pair:
+                    put(p, 4)
+                    put(p, 6)
+        return carry
+    lax.fori_loop(0, 64, two, 0)
 
 
 def source_at(fields, k, x, t):

time: 48.6 us -> 47.8 us (0.984)
  Pallas kernels: 47.4 us -> 46.7 us
    pallas_call x1, Pallas kernels: 3.06 us -> 2.36 us  [local(): pl.pallas_call(source_kernel, out_shape=[field, field], in_specs=[vmem, a...]
where the time goes in v3:
time: 47.8 us; the launch traced here: 47.3 us
  Pallas kernels  46.7 us (98%)
  between operations  0.66 us (1%)
    pallas_call x1, Pallas kernels, local(): pl.pallas_call(step_kernel, out_shape=[tile, tile, tile, tile, tile, halo...  25.9 us
    pallas_call x1, Pallas kernels, local(): pl.pallas_call(first_kernel, out_shape=[tile, tile, tile, tile, tile, til...  15.6 us
    pallas_call x1, Pallas kernels, local(): pl.pallas_call(last_kernel, out_shape=(whole, whole, whole), in_specs=[vm...  2.8 us
    pallas_call x1, Pallas kernels, local(): pl.pallas_call(source_kernel, out_shape=[field, field], in_specs=[vmem, a...  2.36 us

profile of v3, /device:TPU:3, one launch (start us, length us, event | category | flops | bytes accessed | tf_op | source)
XLA Modules:
  0.0 47.3 jit_solution(15594712754800503143)
XLA Ops:
  0.6 15.6 %shard_map.103 = (f32[32,64,256]{2,1,0:T(8,128)S(1)}, f32[32,64,256]{2,1,0:T(8,128)S(1)}, f32[32,64,256]{2,1,0:T(8,128)S(1)}, f32[32,64,256]{2,1,0:T(8,128)S(1)}...) custom-call(f32[32,64,256]{2,1,0:T(8,128)} %current.1, ...), custom_call_target="tpu_custom_call" | custom-call | tf_op jit(solution)/shard_map/pallas_call | solution.py:621
  16.2 2.4 %shard_map.104 = (f32[4096,4,128]{2,1,0:T(4,128)S(1)}, f32[4096,4,128]{2,1,0:T(4,128)S(1)}) custom-call(f32[32,128]{1,0:T(8,128)S(1)} %get-tuple-element.34.values, s32[24,128]{1,0:T(8,128)S(1)} %get-tuple-element.35.targets, f32[4096,4,128]{2,1,0:T(4,128)S(1)} %get-tuple-element.36.blank_a, ...), custom_call_target="tpu_custom_call", output_to_operand_aliasing={{0}: (2, {}), {1}: (3, {})} | custom-call | tf_op jit(solution)/shard_map/pallas_call | solution.py:642
  18.6 25.9 %shard_map.105 = (f32[32,64,256]{2,1,0:T(8,128)S(1)}, f32[32,64,256]{2,1,0:T(8,128)S(1)}, f32[32,64,256]{2,1,0:T(8,128)S(1)}, f32[32,64,256]{2,1,0:T(8,128)S(1)}...) custom-call(f32[32,64,256]{2,1,0:T(8,128)S(1)} %get-tuple-element.27.cur, ...), custom_call_target="tpu_custom_call" | custom-call | tf_op jit(solution)/shard_map/pallas_call | solution.py:656
  44.5 2.8 %shard_map.106 = (f32[32,64,256]{2,1,0:T(8,128)}, f32[32,64,256]{2,1,0:T(8,128)}, f32[32,64,256]{2,1,0:T(8,128)}) custom-call(f32[32,64,256]{2,1,0:T(8,128)S(1)} %get-tuple-element.45.now2, f32[32,64,256]{2,1,0:T(8,128)S(1)} %get-tuple-element.46.now3, f32[32,64,256]{2,1,0:T(8,128)S(1)} %get-tuple-element.47.now4_in, ...), custom_call_target="tpu_custom_call" | custom-call | tf_op jit(solution)/shard_map/pallas_call | solution.py:669
